TPU v7x, 32 devices: a whole 2x2x4 slice. The times are simulated.
32 devices in a mesh: row: 4 (over z), col: 8 (over y, x, core).
Axes of the slice: x: 2, y: 2, z: 4, core: 2. Of those that a mesh axis runs over, the one named last changes fastest.
Arguments:
- blocks: bfloat16 [4, 8, 128, 4096], P('row', 'col'), may hold values from -0.25 to 0.25
- block_row: int32 [4, 8, 128], P('row', 'col'), may hold values from 0 to 15
- block_col: int32 [4, 8, 128], P('row', 'col'), may hold values from 0 to 7
- counts: int32 [4, 8], P('row', 'col'), may hold values from 0 to 128, as said below
- vectors: float32 [64, 4096], P(('col', 'row')), may hold values from -6 to 6
- row_mass: float32 [64, 64], P(('row', 'col')), may hold values from 0.25 to 4
- col_mass: float32 [64, 64], P(('col', 'row')), may hold values from 0.25 to 4
Outputs:
- subspace: float32 [64, 4096], P(('col', 'row'))
Inputs may be any that keep to these rules, and one draw needn't show every extreme that they name: `counts`: in every row panel one tile uses all 128 slots; every other tile uses at most 8.
All inputs are finite; a program needn't handle non-finite values.
Results may differ from a plain program's by a relative error of at most 0.0085.
Values may be sent and summed in bfloat16 or wider, within the bound.
No kernel may reach another device: no remote copies, remote signals or barrier semaphores. Data moves between devices by JAX's collectives and lax.ppermute only.
A program may use at most 64 MiB of HBM per device.

v0:
```python
import jax
import jax.numpy as jnp
from jax import lax
from jax.sharding import PartitionSpec as P

ITERS = 4


def rotate(projected, gram):
    lower = jnp.linalg.cholesky(gram)
    inverse = lax.linalg.triangular_solve(
        lower, jnp.eye(gram.shape[0], dtype=jnp.float32), left_side=True, lower=True
    )
    return jnp.einsum(
        "kl,bli->bki",
        inverse,
        projected,
        precision=lax.Precision.HIGHEST,
        preferred_element_type=jnp.float32,
    )


def local_gram(projected):
    return jnp.einsum(
        "bki,bli->kl",
        projected,
        projected,
        precision=lax.Precision.HIGHEST,
        preferred_element_type=jnp.float32,
    )


def per_device(blocks, block_row, block_col, counts, vectors, row_mass, col_mass):
    tile = blocks[0, 0]
    n_cap = tile.shape[0]
    bsize = row_mass.shape[1]
    vecs = vectors.shape[1] // bsize
    own = vectors.shape[0]
    n_row = lax.axis_size("row")
    n_col = lax.axis_size("col")
    row_panel = own * n_col
    col_panel = own * n_row
    total_boxes = float(own * bsize * n_row * n_col)
    rows_idx = block_row[0, 0]
    cols_idx = block_col[0, 0]
    live = jnp.arange(n_cap) < counts[0, 0]
    fwd_ids = jnp.where(live, rows_idx, row_panel)
    bwd_ids = jnp.where(live, cols_idx, col_panel)
    square = tile.reshape(n_cap, bsize, bsize)
    inv_col = 1.0 / jnp.sqrt(col_mass)
    current = vectors.reshape(own, vecs, bsize)
    for step in range(ITERS):
        scaled = (current * inv_col[:, None, :]).astype(jnp.bfloat16).reshape(own, vecs * bsize)
        panel = lax.all_gather(scaled, "row", axis=0, tiled=True)
        forward_taken = jnp.take(panel.reshape(col_panel, vecs, bsize), cols_idx, axis=0)
        forward_product = jnp.einsum(
            "bij,bkj->bki", square, forward_taken, preferred_element_type=jnp.float32
        )
        forward_summed = jax.ops.segment_sum(forward_product, fwd_ids, num_segments=row_panel + 1)
        rows_sum = lax.psum_scatter(
            forward_summed[:row_panel].reshape(row_panel, vecs * bsize),
            "col",
            scatter_dimension=0,
            tiled=True,
        )
        weighted = (rows_sum.reshape(own, vecs, bsize) * row_mass[:, None, :]).astype(jnp.bfloat16)
        whole_rows = lax.all_gather(weighted.reshape(own, vecs * bsize), "col", axis=0, tiled=True)
        taken = jnp.take(whole_rows.reshape(row_panel, vecs, bsize), rows_idx, axis=0)
        product = jnp.einsum("bij,bki->bkj", square, taken, preferred_element_type=jnp.float32)
        summed = jax.ops.segment_sum(product, bwd_ids, num_segments=col_panel + 1)
        cols_sum = lax.psum_scatter(
            summed[:col_panel].reshape(col_panel, vecs * bsize),
            "row",
            scatter_dimension=0,
            tiled=True,
        )
        projected = cols_sum.reshape(own, vecs, bsize) * inv_col[:, None, :]
        gram = lax.psum(local_gram(projected), ("row", "col")) / total_boxes
        current = rotate(projected, gram)
    return current.reshape(own, vecs * bsize)


def solution(mesh):
    in_specs = (
        P("row", "col", None, None),
        P("row", "col", None),
        P("row", "col", None),
        P("row", "col"),
        P(("col", "row"), None),
        P(("row", "col"), None),
        P(("col", "row"), None),
    )
    out_specs = P(("col", "row"), None)
    return jax.shard_map(
        per_device, mesh=mesh, in_specs=in_specs, out_specs=out_specs, check_vma=False
    )
```

profile of v0, /device:TPU:0, one launch (start us, length us, event | category | flops | bytes accessed | tf_op | source)
XLA Modules:
  0.0 858.6 jit_solution(6217608287064874365)
XLA Ops:
  9.4 14.9 %all-gather = bf16[4,2,4096]{2,1,0:T(2,128)(2,1)S(1)} all-gather(bf16[1,2,4096]{2,1,0:T(2,128)(2,1)S(1)} %fusion.66), channel_id=1, replica_groups=mesh['row'=4,'col'=8] {'row'}, dimensions={0}, use_global_device_ids=true | all-gather | bytes 81920 | tf_op jit(solution)/shard_map/all_gather | solution.py:54
  26.1 3.0 copy.49
  29.8 2.1 gather_fusion
  31.9 4.8 fusion.14
  36.8 13.6 %scatter_fusion = f32[17,64,64]{2,1,0:T(8,128)S(1)} fusion(f32[17,64,64]{2,1,0:T(8,128)S(1)} %broadcast.95.clone.2, s32[128]{0:T(128)S(1)} %get-tuple-element.18, f32[128,64,64]{2,1,0:T(8,128)} %fusion.14), kind=kCustom, calls=%fused_computation.8 | custom fusion | flops 524288 | bytes 6291968 | tf_op jit(solution)/shard_map/scatter-add | solution.py:59
  52.9 53.4 %all-reduce.17.cloned.1.call-done = f32[16,4096]{1,0:T(8,128)} async-done(((f32[16,4096]{1,0:T(8,128)}), f32[16,4096]{1,0:T(8,128)}) %all-reduce.17.cloned.1.call-update) | async-done | bytes 262160
  107.2 8.5 all-gather.1
  115.9 2.1 gather_fusion.1
  118.0 4.3 fusion.12
  122.4 13.6 %scatter_fusion.1 = f32[9,64,64]{2,1,0:T(8,128)S(1)} fusion(f32[9,64,64]{2,1,0:T(8,128)S(1)} %broadcast.94.clone.2, s32[128]{0:T(128)S(1)} %get-tuple-element.17, f32[128,64,64]{2,1,0:T(8,128)} %fusion.12), kind=kCustom, calls=%fused_computation.9 | custom fusion | flops 524288 | bytes 6291968 | tf_op jit(solution)/shard_map/scatter-add | solution.py:70
  138.1 33.3 %all-reduce.19.cloned.1.call-done = f32[8,4096]{1,0:T(8,128)} async-done(((f32[8,4096]{1,0:T(8,128)}), f32[8,4096]{1,0:T(8,128)}) %all-reduce.19.cloned.1.call-update) | async-done | bytes 131088
  172.7 40.2 %psum.28 = f32[64,64]{0,1:T(8,128)S(1)} all-reduce(f32[64,64]{0,1:T(8,128)S(1)} %convolution_bitcast_fusion.8), channel_id=1, replica_groups=mesh['row'=4,'col'=8] {'row','col'}, use_global_device_ids=true, to_apply=%region_4.7 | all-reduce | flops 4096 | bytes 32768 | tf_op jit(solution)/shard_map/psum | solution.py:78
  213.0 5.8 cholesky.74
  220.2 4.9 custom-call.8
  226.0 13.4 %all-gather.2 = bf16[4,2,4096]{2,1,0:T(2,128)(2,1)S(1)} all-gather(bf16[1,2,4096]{2,1,0:T(2,128)(2,1)S(1)} %reshape.324), channel_id=1, replica_groups=mesh['row'=4,'col'=8] {'row'}, dimensions={0}, use_global_device_ids=true | all-gather | bytes 81920 | tf_op jit(solution)/shard_map/all_gather | solution.py:54
  239.6 2.1 gather_fusion.2
  241.7 4.8 fusion.10
  246.5 13.6 %scatter_fusion.2 = f32[17,64,64]{2,1,0:T(8,128)S(1)} fusion(f32[17,64,64]{2,1,0:T(8,128)S(1)} %broadcast.95.clone.1, s32[128]{0:T(128)S(1)} %get-tuple-element.18, f32[128,64,64]{2,1,0:T(8,128)} %fusion.10), kind=kCustom, calls=%fused_computation.10 | custom fusion | flops 524288 | bytes 6291968 | tf_op jit(solution)/shard_map/scatter-add | solution.py:59
  261.2 53.2 %all-reduce.21.cloned.1.call-done = f32[16,4096]{1,0:T(8,128)} async-done(((f32[16,4096]{1,0:T(8,128)}), f32[16,4096]{1,0:T(8,128)}) %all-reduce.21.cloned.1.call-update) | async-done | bytes 262160
  315.3 8.5 all-gather.3
  326.2 4.3 fusion.8
  330.5 13.6 %scatter_fusion.3 = f32[9,64,64]{2,1,0:T(8,128)S(1)} fusion(f32[9,64,64]{2,1,0:T(8,128)S(1)} %broadcast.94.clone.1, s32[128]{0:T(128)S(1)} %get-tuple-element.17, f32[128,64,64]{2,1,0:T(8,128)} %fusion.8), kind=kCustom, calls=%fused_computation.11 | custom fusion | flops 524288 | bytes 6291968 | tf_op jit(solution)/shard_map/scatter-add | solution.py:70
  345.0 34.6 %all-reduce.23.cloned.1.call-done = f32[8,4096]{1,0:T(8,128)} async-done(((f32[8,4096]{1,0:T(8,128)}), f32[8,4096]{1,0:T(8,128)}) %all-reduce.23.cloned.1.call-update) | async-done | bytes 131088
  380.9 40.2 %psum.29 = f32[64,64]{0,1:T(8,128)S(1)} all-reduce(f32[64,64]{0,1:T(8,128)S(1)} %convolution_bitcast_fusion.6), channel_id=1, replica_groups=mesh['row'=4,'col'=8] {'row','col'}, use_global_device_ids=true, to_apply=%region_11.16 | all-reduce | flops 4096 | bytes 32768 | tf_op jit(solution)/shard_map/psum | solution.py:78
  421.2 5.8 cholesky.85
  428.4 4.9 custom-call.9
  434.2 13.2 %all-gather.4 = bf16[4,2,4096]{2,1,0:T(2,128)(2,1)S(1)} all-gather(bf16[1,2,4096]{2,1,0:T(2,128)(2,1)S(1)} %reshape.328), channel_id=1, replica_groups=mesh['row'=4,'col'=8] {'row'}, dimensions={0}, use_global_device_ids=true | all-gather | bytes 81920 | tf_op jit(solution)/shard_map/all_gather | solution.py:54
  449.7 4.8 fusion.6
  454.6 13.6 %scatter_fusion.4 = f32[17,64,64]{2,1,0:T(8,128)S(1)} fusion(f32[17,64,64]{2,1,0:T(8,128)S(1)} %broadcast.95.clone, s32[128]{0:T(128)S(1)} %get-tuple-element.18, f32[128,64,64]{2,1,0:T(8,128)} %fusion.6), kind=kCustom, calls=%fused_computation.12 | custom fusion | flops 524288 | bytes 6291968 | tf_op jit(solution)/shard_map/scatter-add | solution.py:59
  469.2 53.2 %all-reduce.25.cloned.1.call-done = f32[16,4096]{1,0:T(8,128)} async-done(((f32[16,4096]{1,0:T(8,128)}), f32[16,4096]{1,0:T(8,128)}) %all-reduce.25.cloned.1.call-update) | async-done | bytes 262160
  523.4 8.7 %all-gather.5 = bf16[8,2,4096]{2,1,0:T(2,128)(2,1)S(1)} all-gather(bf16[1,2,4096]{2,1,0:T(2,128)(2,1)S(1)} %fusion.69), channel_id=1, replica_groups=mesh['row'=4,'col'=8] {'col'}, dimensions={0}, use_global_device_ids=true | all-gather | bytes 147456 | tf_op jit(solution)/shard_map/all_gather | solution.py:67
  534.5 4.3 fusion.4
  538.8 13.6 %scatter_fusion.5 = f32[9,64,64]{2,1,0:T(8,128)S(1)} fusion(f32[9,64,64]{2,1,0:T(8,128)S(1)} %broadcast.94.clone, s32[128]{0:T(128)S(1)} %get-tuple-element.17, f32[128,64,64]{2,1,0:T(8,128)} %fusion.4), kind=kCustom, calls=%fused_computation.13 | custom fusion | flops 524288 | bytes 6291968 | tf_op jit(solution)/shard_map/scatter-add | solution.py:70
  553.3 34.6 %all-reduce.27.cloned.1.call-done = f32[8,4096]{1,0:T(8,128)} async-done(((f32[8,4096]{1,0:T(8,128)}), f32[8,4096]{1,0:T(8,128)}) %all-reduce.27.cloned.1.call-update) | async-done | bytes 131088
  589.1 40.2 %psum.30 = f32[64,64]{0,1:T(8,128)S(1)} all-reduce(f32[64,64]{0,1:T(8,128)S(1)} %convolution_bitcast_fusion.4), channel_id=1, replica_groups=mesh['row'=4,'col'=8] {'row','col'}, use_global_device_ids=true, to_apply=%region_16.21 | all-reduce | flops 4096 | bytes 32768 | tf_op jit(solution)/shard_map/psum | solution.py:78
  629.5 5.8 cholesky.96
  636.6 4.9 custom-call.10
  642.5 13.2 %all-gather.6 = bf16[4,2,4096]{2,1,0:T(2,128)(2,1)S(1)} all-gather(bf16[1,2,4096]{2,1,0:T(2,128)(2,1)S(1)} %reshape.332), channel_id=1, replica_groups=mesh['row'=4,'col'=8] {'row'}, dimensions={0}, use_global_device_ids=true | all-gather | bytes 81920 | tf_op jit(solution)/shard_map/all_gather | solution.py:54
  658.0 4.8 fusion.2
  662.8 13.6 %scatter_fusion.6 = f32[17,64,64]{2,1,0:T(8,128)S(1)} fusion(f32[17,64,64]{2,1,0:T(8,128)S(1)} %broadcast.95, s32[128]{0:T(128)S(1)} %get-tuple-element.18, f32[128,64,64]{2,1,0:T(8,128)} %fusion.2), kind=kCustom, calls=%fused_computation.14 | custom fusion | flops 524288 | bytes 6291968 | tf_op jit(solution)/shard_map/scatter-add | solution.py:59
  677.4 53.2 %all-reduce.29.cloned.1.call-done = f32[16,4096]{1,0:T(8,128)} async-done(((f32[16,4096]{1,0:T(8,128)}), f32[16,4096]{1,0:T(8,128)}) %all-reduce.29.cloned.1.call-update) | async-done | bytes 262160
  731.6 8.5 all-gather.7
  742.5 4.3 fusion
  746.8 13.6 %scatter_fusion.7 = f32[9,64,64]{2,1,0:T(8,128)S(1)} fusion(f32[9,64,64]{2,1,0:T(8,128)S(1)} %broadcast.94, s32[128]{0:T(128)S(1)} %get-tuple-element.17, f32[128,64,64]{2,1,0:T(8,128)} %fusion), kind=kCustom, calls=%fused_computation.15 | custom fusion | flops 524288 | bytes 6291968 | tf_op jit(solution)/shard_map/scatter-add | solution.py:70
  761.2 34.6 %all-reduce.31.cloned.1.call-done = f32[8,4096]{1,0:T(8,128)} async-done(((f32[8,4096]{1,0:T(8,128)}), f32[8,4096]{1,0:T(8,128)}) %all-reduce.31.cloned.1.call-update) | async-done | bytes 131088
  797.1 40.5 %psum.31 = f32[64,64]{0,1:T(8,128)S(1)} all-reduce(f32[64,64]{0,1:T(8,128)S(1)} %convolution_bitcast_fusion.2), channel_id=1, replica_groups=mesh['row'=4,'col'=8] {'row','col'}, use_global_device_ids=true, to_apply=%region_21.26 | all-reduce | flops 4096 | bytes 32768 | tf_op jit(solution)/shard_map/psum | solution.py:78
  837.7 5.8 cholesky.107
  844.9 4.9 custom-call.11
  (143 shorter events, 44.0 us)
Async XLA Ops:
  6.5 99.7 %all-reduce.17.cloned.1.call-start = ((), (), s32[]{:S(2)}) async-start(), calls=%async_computation | async-start | bytes 524288
  29.8 2.2 copy-start.1
  29.8 2.2 copy-start.2
  50.4 1.1 copy-start
  50.4 1.2 copy-start.4
  51.4 120.0 %all-reduce.19.cloned.1.call-start = ((), (), s32[]{:S(2)}) async-start(), calls=%async_computation.1 | async-start | bytes 262144
  122.3 14.5 %copy-start.3 = (u32[32]{0:T(128)S(1)}, u32[32]{0:T(128)}, u32[]{:S(2)}) copy-start(u32[32]{0:T(128)} %constant.76) | copy-start | bytes 388
  136.8 177.6 %all-reduce.21.cloned.1.call-start = ((), (), s32[]{:S(2)}) async-start(), calls=%async_computation.2 | async-start | bytes 524288
  261.1 118.5 %all-reduce.23.cloned.1.call-start = ((), (), s32[]{:S(2)}) async-start(), calls=%async_computation.3 | async-start | bytes 262144
  345.0 177.4 %all-reduce.25.cloned.1.call-start = ((), (), s32[]{:S(2)}) async-start(), calls=%async_computation.4 | async-start | bytes 524288
  469.1 118.7 %all-reduce.27.cloned.1.call-start = ((), (), s32[]{:S(2)}) async-start(), calls=%async_computation.5 | async-start | bytes 262144
  553.2 177.5 %all-reduce.29.cloned.1.call-start = ((), (), s32[]{:S(2)}) async-start(), calls=%async_computation.6 | async-start | bytes 524288
  677.4 118.5 %all-reduce.31.cloned.1.call-start = ((), (), s32[]{:S(2)}) async-start(), calls=%async_computation.7 | async-start | bytes 262144
Sparse Core Ops, SparseCore 0:
  51.5 54.6 all-reduce.16
  136.9 34.4 all-reduce.18
  261.2 53.1 all-reduce.20
  345.1 34.4 all-reduce.22
  469.3 53.1 all-reduce.24
  553.3 34.4 all-reduce.26
  677.5 53.1 all-reduce.28
  761.4 34.4 all-reduce.30
where the time goes:
time: 870 us; the launch traced here: 859 us
  waiting for transfers between devices  350 us (40%)
  blocking collectives  250 us (29%)
  other arithmetic  167 us (19%)
  matrix products  39.1 us (4%)
  local copies, waits for them, and re-layouts  35.2 us (4%)
  between operations  16.6 us (2%)
    unnamed x16, waiting for transfers between devices  350 us
    psum x4, blocking collectives, per_device(): gram = lax.psum(local_gram(projected), ('row', 'col')) / total_boxes  161 us
    all_gather x4, blocking collectives, per_device(): panel = lax.all_gather(scaled, 'row', axis=0, tiled=True)  54.6 us
    scatter-add x4, other arithmetic, per_device(): summed = jax.ops.segment_sum(product, bwd_ids, num_segments=col_panel + 1)  54.5 us
    scatter-add x4, other arithmetic, per_device(): jax.ops.segment_sum(forward_product, fwd_ids, num_segments=row_panel + 1)  54.5 us
    all_gather x4, blocking collectives, per_device(): lax.all_gather(weighted.reshape(own, vecs * bsize), 'col', axis=0, tiled=...  34.3 us
    another operation x12, other arithmetic, rotate(): lower = jnp.linalg.cholesky(gram)  26.1 us
    another operation x8, other arithmetic, rotate(): lax.linalg.triangular_solve(lower, jnp.eye(gram.shape[0], dtype=jnp.float...  22.2 us
  transfers between devices with their start and end apart: 8, of which 8 were waited for; matrix products, arithmetic and copies ran while one was open for 0% of the time, Pallas kernels for 0%

commit v1 on v0

--- a/solution.py
+++ b/solution.py
@@ -1,9 +1,295 @@
+import functools
+
 import jax
 import jax.numpy as jnp
 from jax import lax
+from jax.experimental import pallas as pl
+from jax.experimental.pallas import tpu as pltpu
 from jax.sharding import PartitionSpec as P
 
 ITERS = 4
+OFF_CAP = 8
+META = 16
+UNROLL = 4
+VMEM_LIMIT = 56 * 1024 * 1024
+
+NT = (((1,), (1,)), ((), ()))
+NN = (((1,), (0,)), ((), ()))
+
+
+def dot(a, b, dims=NN):
+    return lax.dot_general(a, b, dims, preferred_element_type=jnp.float32)
+
+
+def split2(x):
+    hi = x.astype(jnp.bfloat16)
+    return hi, (x - hi.astype(jnp.float32)).astype(jnp.bfloat16)
+
+
+def inverse_factor(gram):
+    n = gram.shape[0]
+    rows = lax.broadcasted_iota(jnp.int32, (n, n), 0)
+    cols = lax.broadcasted_iota(jnp.int32, (n, n), 1)
+    eye = (rows == cols).astype(jnp.float32)
+    both = jnp.concatenate([gram, eye], axis=1)
+    tiles = [both[8 * t : 8 * t + 8] for t in range(n // 8)]
+    sub = lax.broadcasted_iota(jnp.int32, (8, 2 * n), 0)
+    lane = lax.broadcasted_iota(jnp.int32, (8, 2 * n), 1)
+    for j in range(n):
+        t0, s0 = divmod(j, 8)
+        row = tiles[t0][s0 : s0 + 1]
+        step = row * (1.0 / row[:, j : j + 1])
+        for t in range(t0, n // 8):
+            factor = jnp.broadcast_to(tiles[t][:, j : j + 1], (8, 2 * n))
+            if t == t0:
+                factor = jnp.where(sub > s0, factor, 0.0)
+            tiles[t] = tiles[t] - factor * step
+    out = []
+    for t in range(n // 8):
+        pivot = jnp.sum(jnp.where(lane == sub + 8 * t, tiles[t], 0.0), axis=1, keepdims=True)
+        out.append(tiles[t] * lax.rsqrt(pivot))
+    return jnp.concatenate(out, axis=0)[:, n:]
+
+
+def kernel(
+    n_row, n_col, n_cap, total,
+    meta, own, pay, out,
+    lv, lw, tmp, home, emb, vs, w, wt, y, ph, rm, ic, linv,
+):
+    n_dev = n_row * n_col
+    k = vs.shape[1]
+    half = k // 2
+    rpairs, cpairs = n_col, n_row
+    rblk = 2 * rpairs
+    part = n_cap // n_col
+    off_at = half * part
+    vec_at = off_at + OFF_CAP * half
+    meta_at = vec_at + k
+    width = cpairs * 128
+    height = rblk * k
+
+    left = lax.broadcasted_iota(jnp.int32, (rblk, 128), 1) < 64
+
+    for r in range(n_row):
+        for c in range(n_col):
+            q, p = c * n_row + r, r * n_col + c
+            rows = pay[q, meta_at : meta_at + META, :].astype(jnp.float32)
+            rm[p] = jnp.broadcast_to(rows[0:1] + rows[1:2] + rows[2:3], (8, 128))
+            ic[q] = jnp.broadcast_to(rows[3:4] + rows[4:5] + rows[5:6], (8, 128))
+            vs[q] = pay[q, vec_at : vec_at + k, :]
+
+    homes = []
+    for r in range(n_row):
+        h = jnp.int32(0)
+        for c in range(n_col):
+            h = jnp.where(meta[c * n_row + r, 2 * OFF_CAP] > OFF_CAP, c, h)
+        homes.append(h)
+        index = pay[h * n_row + r, meta_at : meta_at + META, :].astype(jnp.float32)
+        place = index[7:8] * float(rblk) + index[6:7]
+        want = lax.broadcasted_iota(jnp.int32, (2 * cpairs * rblk, n_cap), 0).astype(jnp.float32)
+        select = jnp.where(want == place, 1.0, 0.0).astype(jnp.bfloat16)
+
+        def build(m, carry, r=r, select=select):
+            at = pl.multiple_of(m * part, part)
+            slots = jnp.concatenate(
+                [pay[c * n_row + r, pl.ds(at, part), :] for c in range(n_col)], axis=0
+            )
+            dense = dot(select, slots)
+            for u in range(cpairs):
+                a = dense[2 * u * rblk : (2 * u + 1) * rblk]
+                b = dense[(2 * u + 1) * rblk : (2 * u + 2) * rblk]
+                even = jnp.where(left, a, pltpu.roll(b, 64, 1))
+                odd = jnp.where(left, pltpu.roll(a, 64, 1), b)
+                tmp[u, pl.ds(m, rblk, stride=k), :] = even
+                tmp[u, pl.ds(m + half, rblk, stride=k), :] = odd
+            return carry
+
+        lax.fori_loop(0, half, build, 0, unroll=2)
+
+        def cut(i, carry, r=r):
+            at = pl.multiple_of(i * k, k)
+            for u in range(cpairs):
+                hi, lo = split2(tmp[u, pl.ds(at, k), :])
+                home[r, pl.ds(at, k), u * 128 : (u + 1) * 128] = hi
+                home[r, pl.ds(at, k), width + u * 128 : width + (u + 1) * 128] = lo
+            return carry
+
+        lax.fori_loop(0, rblk, cut, 0, unroll=2)
+
+    lanes = lax.broadcasted_iota(jnp.int32, (half, 128), 1)
+
+    def device(q, n):
+        count = meta[q, 2 * OFF_CAP]
+        count = jnp.where(count > OFF_CAP, 0, count)
+        c = q // n_row
+        r = q - c * n_row
+
+        def slot(s, n):
+            br, bc = meta[q, s], meta[q, OFF_CAP + s]
+            lv[n] = c * cpairs + bc // 2
+            lw[n] = r * rpairs + br // 2
+            side, row = bc % 2, pl.multiple_of((br % 2) * k, k)
+            other = pl.multiple_of(k - row, k)
+            at = pl.multiple_of(off_at + s * half, half)
+            x = pay[q, pl.ds(at, half), :].astype(jnp.float32)
+            rolled = pltpu.roll(x, 64, 1)
+            mask = (lanes // 64) == side
+            even = jnp.where(mask, jnp.where(side == 0, x, rolled), 0.0)
+            odd = jnp.where(mask, jnp.where(side == 0, rolled, x), 0.0)
+            block = jnp.concatenate([even, odd], axis=0).astype(jnp.bfloat16)
+            emb[n, pl.ds(row, k), :] = block
+            emb[n, pl.ds(other, k), :] = jnp.zeros_like(block)
+            return n + 1
+
+        return lax.fori_loop(0, count, slot, n)
+
+    n_live = lax.fori_loop(0, n_dev, device, jnp.int32(0))
+    for u in range(UNROLL - 1):
+        lv[n_live + u] = 0
+        lw[n_live + u] = 0
+        emb[n_live + u] = jnp.zeros((128, 128), jnp.bfloat16)
+    n_group = (n_live + UNROLL - 1) // UNROLL
+
+    def iteration(it, carry):
+        @pl.when(it > 0)
+        def _():
+            lh, ll = split2(linv[...])
+            for q in range(n_dev):
+                hi, lo = ph[q, :k, :], ph[q, k:, :]
+                current = dot(lh, hi) + dot(ll, hi) + dot(lh, lo)
+                vs[q] = (current * ic[q, 0:1, :]).astype(jnp.bfloat16)
+
+        for r in range(n_row):
+            base = homes[r] * cpairs
+            vec = jnp.concatenate([vs[base + u] for u in range(cpairs)] * 2, axis=1)
+            for p in range(0, rpairs, 2):
+                prod = dot(vec, home[r, p * 128 : (p + 2) * 128, :], NT)
+                w[r * rpairs + p] = prod[:, :128]
+                w[r * rpairs + p + 1] = prod[:, 128:]
+
+        def forward(i, carry):
+            prods = [dot(vs[lv[i * UNROLL + u]], emb[i * UNROLL + u], NT) for u in range(UNROLL)]
+            for u in range(UNROLL):
+                p = lw[i * UNROLL + u]
+                w[p] = w[p] + prods[u]
+            return carry
+
+        lax.fori_loop(0, n_group, forward, 0)
+        for p in range(n_dev):
+            wt[p] = (w[p] * rm[p, 0:1, :]).astype(jnp.bfloat16)
+            y[p] = jnp.zeros_like(y[p])
+
+        for r in range(n_row):
+            base = homes[r] * cpairs
+            vec = jnp.concatenate([wt[r * rpairs + p] for p in range(rpairs)], axis=1)
+            for u in range(0, cpairs, 2):
+                cols = slice(u * 128, (u + 2) * 128)
+                tail = slice(width + u * 128, width + (u + 2) * 128)
+                prod = dot(vec, home[r, :, cols]) + dot(vec, home[r, :, tail])
+                y[base + u] = y[base + u] + prod[:, :128]
+                y[base + u + 1] = y[base + u + 1] + prod[:, 128:]
+
+        def backward(i, carry):
+            prods = [dot(wt[lw[i * UNROLL + u]], emb[i * UNROLL + u]) for u in range(UNROLL)]
+            for u in range(UNROLL):
+                q = lv[i * UNROLL + u]
+                y[q] = y[q] + prods[u]
+            return carry
+
+        lax.fori_loop(0, n_group, backward, 0)
+
+        both = jnp.zeros((2 * k, k), jnp.float32)
+        for q in range(0, n_dev, 4):
+            his, los = [], []
+            for d in range(4):
+                hi, lo = split2(y[q + d] * ic[q + d, 0:1, :])
+                ph[q + d, :k, :] = hi
+                ph[q + d, k:, :] = lo
+                his.append(hi)
+                los.append(lo)
+            hi = jnp.concatenate(his, axis=1)
+            lo = jnp.concatenate(los, axis=1)
+            both = both + dot(jnp.concatenate([hi, lo], axis=0), hi, NT)
+        gram = (both[:k] + (both[k:] + both[k:].T)) / total
+        linv[...] = inverse_factor(gram)
+        return carry
+
+    lax.fori_loop(0, ITERS, iteration, 0)
+    lh, ll = split2(linv[...])
+    hi, lo = ph[own[0], :k, :], ph[own[0], k:, :]
+    out[...] = dot(lh, hi) + dot(ll, hi) + dot(lh, lo)
+
+
+def split3(x):
+    a = lax.reduce_precision(x, 8, 7)
+    b = lax.reduce_precision(x - a, 8, 7)
+    return [v.astype(jnp.bfloat16) for v in (a, b, x - a - b)]
+
+
+def whole_on_each(n_row, n_col, blocks, block_row, block_col, counts, vectors, row_mass, col_mass):
+    tile = blocks[0, 0]
+    n_cap = tile.shape[0]
+    own, bsize = row_mass.shape
+    k = vectors.shape[1] // bsize
+    half = bsize // 2
+    part = n_cap // n_col
+    n_dev = n_row * n_col
+    count = counts[0, 0]
+    full = count > OFF_CAP
+    bf16 = jnp.bfloat16
+
+    sent = jnp.where(full, tile, jnp.zeros_like(tile)).reshape(n_col, part, bsize * bsize)
+    got = lax.all_to_all(sent, "col", split_axis=0, concat_axis=0)
+    home = jnp.sum(got.astype(jnp.float32), axis=0).astype(bf16)
+    home = home.reshape(part, half, 128).transpose(1, 0, 2).reshape(half * part, 128)
+    off = tile[:OFF_CAP].reshape(OFF_CAP * half, 128)
+
+    inv_col = 1.0 / jnp.sqrt(col_mass)
+    scaled = (vectors.reshape(own, k, bsize) * inv_col[:, None, :]).astype(bf16)
+    scaled = scaled.transpose(1, 0, 2).reshape(k, own * bsize)
+    mass = row_mass.reshape(own, half, 2).transpose(0, 2, 1).reshape(own * bsize)
+    rows, cols = block_row[0, 0], block_col[0, 0]
+    small = jnp.concatenate(
+        [rows[:OFF_CAP], cols[:OFF_CAP], count[None], jnp.zeros(128 - 2 * OFF_CAP - 1, jnp.int32)]
+    )
+    meta = [v.astype(bf16) for v in (rows, cols, small)]
+    meta = split3(mass) + split3(inv_col.reshape(own * bsize)) + meta
+    meta = jnp.stack(meta + [jnp.zeros(128, bf16)] * (META - len(meta)))
+    payload = jnp.concatenate([home, off, scaled, meta], axis=0)
+    pay = lax.all_gather(payload, ("col", "row"), axis=0)
+    ints = pay[:, payload.shape[0] - META + 8, :32].astype(jnp.int32)
+    place = lax.axis_index("col") * n_row + lax.axis_index("row")
+
+    height, width = 2 * n_col * bsize, 2 * n_row * bsize
+    slots = n_dev * OFF_CAP + UNROLL
+    result = pl.pallas_call(
+        functools.partial(kernel, n_row, n_col, n_cap, float(n_dev * own * bsize)),
+        out_shape=jax.ShapeDtypeStruct((k, 128), jnp.float32),
+        in_specs=[
+            pl.BlockSpec(memory_space=pltpu.SMEM),
+            pl.BlockSpec(memory_space=pltpu.SMEM),
+            pl.BlockSpec(memory_space=pltpu.VMEM),
+        ],
+        out_specs=pl.BlockSpec(memory_space=pltpu.VMEM),
+        scratch_shapes=[
+            pltpu.SMEM((slots,), jnp.int32),
+            pltpu.SMEM((slots,), jnp.int32),
+            pltpu.VMEM((n_row, height, 128), jnp.float32),
+            pltpu.VMEM((n_row, height, 2 * width), bf16),
+            pltpu.VMEM((slots, 128, 128), bf16),
+            pltpu.VMEM((n_dev, k, 128), bf16),
+            pltpu.VMEM((n_dev, k, 128), jnp.float32),
+            pltpu.VMEM((n_dev, k, 128), bf16),
+            pltpu.VMEM((n_dev, k, 128), jnp.float32),
+            pltpu.VMEM((n_dev, 2 * k, 128), bf16),
+            pltpu.VMEM((n_dev, 8, 128), jnp.float32),
+            pltpu.VMEM((n_dev, 8, 128), jnp.float32),
+            pltpu.VMEM((k, k), jnp.float32),
+        ],
+        compiler_params=pltpu.CompilerParams(vmem_limit_bytes=VMEM_LIMIT),
+        name="iterate",
+    )(ints, place[None].astype(jnp.int32), pay)
+    return result.reshape(k, own, bsize).transpose(1, 0, 2).reshape(own, k * bsize)
 
 
 def rotate(projected, gram):
@@ -30,7 +316,7 @@
     )
 
 
-def per_device(blocks, block_row, block_col, counts, vectors, row_mass, col_mass):
+def split_by_tile(blocks, block_row, block_col, counts, vectors, row_mass, col_mass):
     tile = blocks[0, 0]
     n_cap = tile.shape[0]
     bsize = row_mass.shape[1]
@@ -80,6 +366,17 @@
     return current.reshape(own, vecs * bsize)
 
 
+def per_device(blocks, block_row, block_col, counts, vectors, row_mass, col_mass):
+    n_row, n_col = lax.axis_size("row"), lax.axis_size("col")
+    own, bsize = row_mass.shape
+    n_cap = blocks.shape[2]
+    dense = n_row * (own * n_col * bsize) * (own * n_row * bsize) * 4
+    fits = dense <= VMEM_LIMIT // 4 and own * bsize == 128 and vectors.shape[1] == bsize * bsize
+    fits = fits and n_cap == 128 and n_cap % (16 * n_col) == 0 and n_row % 2 == 0 and n_col % 2 == 0
+    args = (blocks, block_row, block_col, counts, vectors, row_mass, col_mass)
+    return whole_on_each(n_row, n_col, *args) if fits else split_by_tile(*args)
+
+
 def solution(mesh):
     in_specs = (
         P("row", "col", None, None),

time: 870 us -> 238 us (0.27)
  waiting for transfers between devices: 350 us -> 82.8 us
  blocking collectives: 250 us -> 0 us
  other arithmetic: 167 us -> 4.07 us
  Pallas kernels: 0 us -> 119 us
  matrix products: 39.1 us -> 0 us
  local copies, waits for them, and re-layouts: 35.2 us -> 8.34 us
    unnamed x16 -> x1, waiting for transfers between devices: 350 us -> 0.02 us
    psum x4 -> x0, blocking collectives: 161 us -> none  [per_device(): gram = lax.psum(local_gram(projected), ('row', 'col')) / total_boxes]
    pallas_call x0 -> x1, Pallas kernels: none -> 119 us  [whole_on_each(): pl.pallas_call(functools.partial(kernel, n_row, n_col, n_cap, float(n_dev...]
    scatter-add x8 -> x0, other arithmetic: 109 us -> none  [the longest x4 54.5 us: per_device(): summed = jax.ops.segment_sum(product, bwd_ids, num_segments=col_panel + 1)]
    all_gather x8 -> x0, blocking collectives: 89 us -> none  [the longest x4 54.6 us: per_device(): panel = lax.all_gather(scaled, 'row', axis=0, tiled=True)]
    all_gather x0 -> x1, waiting for transfers between devices: none -> 72.5 us  [whole_on_each(): pay = lax.all_gather(payload, ('col', 'row'), axis=0)]
    another operation x20 -> x0, other arithmetic: 48.3 us -> none  [the longest x12 26.1 us: rotate(): lower = jnp.linalg.cholesky(gram)]
    dot_general x16 -> x0, matrix products: 38.1 us -> none  [the longest x4 19.1 us: per_device(): jnp.einsum('bij,bkj->bki', square, forward_taken, preferred_element_type=...]
  transfers between devices with their start and end apart: 8 -> 2, of which waited for: 8 -> 2; matrix products, arithmetic and copies ran while one was open for 0% -> 2% of each run, Pallas kernels for 0% -> 0%
where the time goes in v1:
time: 238 us; the launch traced here: 234 us
  Pallas kernels  119 us (50%)
  waiting for transfers between devices  82.8 us (35%)
  between operations  14.2 us (6%)
  local copies, waits for them, and re-layouts  8.34 us (4%)
  starting transfers between devices  5.21 us (2%)
  other arithmetic  4.07 us (2%)
    pallas_call x1, Pallas kernels, whole_on_each(): pl.pallas_call(functools.partial(kernel, n_row, n_col, n_cap, float(n_dev...  119 us
    all_gather x1, waiting for transfers between devices, whole_on_each(): pay = lax.all_gather(payload, ('col', 'row'), axis=0)  72.5 us
    all_to_all x1, waiting for transfers between devices, whole_on_each(): got = lax.all_to_all(sent, 'col', split_axis=0, concat_axis=0)  10.3 us
    all_to_all x1, starting transfers between devices, whole_on_each(): got = lax.all_to_all(sent, 'col', split_axis=0, concat_axis=0)  5.17 us
  transfers between devices with their start and end apart: 2, of which 2 were waited for; matrix products, arithmetic and copies ran while one was open for 2% of the time, Pallas kernels for 0%

profile of v1, /device:TPU:0, one launch (start us, length us, event | category | flops | bytes accessed | tf_op | source)
XLA Modules:
  0.0 233.9 jit_solution(11201534739124109721)
XLA Ops:
  7.2 1.1 broadcast_select_fusion
  8.2 5.2 %all-to-all-start = ((bf16[8,16,4096]{2,1,0:T(8,128)(2,1)}), bf16[8,16,4096]{2,1,0:T(8,128)(2,1)S(1)}, u32[]{:S(2)}, u32[]{:S(2)}) async-start(bf16[8,16,4096]{2,1,0:T(8,128)(2,1)} %bitcast.1), calls=%async_computation | async-start | bytes 2097152 | tf_op jit(solution)/shard_map/all_to_all | solution.py:242
  13.4 0.0 all-gather.3.cloned.1.call-start
  13.5 0.8 slice.17
  14.3 0.7 sqrt.3
  15.0 0.1 reshape.214
  15.1 0.8 reshape.212
  15.9 0.1 copy.23
  16.0 0.1 reshape.213
  16.0 0.9 reshape.210
  17.0 0.1 reshape.211
  17.1 0.7 fusion.3
  17.8 0.7 fusion.4
  18.4 0.1 bitcast_maximum_fusion
  18.5 10.3 %all-to-all-done = bf16[8,16,4096]{2,1,0:T(8,128)(2,1)S(1)} async-done(((bf16[8,16,4096]{2,1,0:T(8,128)(2,1)}), bf16[8,16,4096]{2,1,0:T(8,128)(2,1)S(1)}, u32[]{:S(2)}, u32[]{:S(2)}) %all-to-all-start) | async-done | bytes 1048608 | tf_op jit(solution)/shard_map/all_to_all | solution.py:242
  28.8 0.1 reduce_sum.12
  29.0 0.1 copy.21
  29.1 3.1 %concatenate.29 = bf16[848,128]{1,0:T(8,128)(2,1)} concatenate(bf16[512,128]{1,0:T(8,128)(2,1)S(1)} %bitcast.30, bf16[256,128]{1,0:T(8,128)(2,1)S(1)} %reshape.209, bf16[64,128]{1,0:T(8,128)(2,1)S(1)} %reshape.211, bf16[1,128]{1,0:T(2,128)(2,1)S(1)} %get-tuple-element.14, bf16[1,128]{1,0:T(2,128)(2,1)S(1)} %get-tuple-element.13, bf16[1,128]{1,0:T(2,128)(2,1)S(1)} %get-tuple-element.12, ...), dimensions={0} | concatenate | bytes 434176 | tf_op jit(solution)/shard_map/concatenate | solution.py:258
  32.2 0.0 all-gather.3.cloned.1.call-update
  32.2 72.5 %all-gather.3.cloned.1.call-done = bf16[27136,128]{1,0:T(8,128)(2,1)} async-done(((bf16[848,128]{1,0:T(8,128)(2,1)}), bf16[27136,128]{1,0:T(8,128)(2,1)}) %all-gather.3.cloned.1.call-update) | async-done | bytes 6946832 | tf_op jit(solution)/shard_map/all_gather | solution.py:259
  104.7 1.5 slice_convert_fusion
  106.2 119.3 %iterate.1 = f32[64,128]{1,0:T(8,128)} custom-call(s32[32,32]{1,0:T(8,128)} %bitcast.33, s32[1]{0:T(128)} %bitcast.12.own, bf16[32,848,128]{2,1,0:T(8,128)(2,1)} %bitcast.27), custom_call_target="tpu_custom_call" | custom-call | tf_op jit(solution)/shard_map/iterate/pallas_call | solution.py:265
  225.5 0.9 reshape.215
  226.4 0.7 reshape.216
  (11 shorter events, 0.1 us)
Async XLA Ops:
  8.2 20.6 %all-to-all-start = ((bf16[8,16,4096]{2,1,0:T(8,128)(2,1)}), bf16[8,16,4096]{2,1,0:T(8,128)(2,1)S(1)}, u32[]{:S(2)}, u32[]{:S(2)}) async-start(bf16[8,16,4096]{2,1,0:T(8,128)(2,1)} %bitcast.1), calls=%async_computation | async-start | bytes 2097152 | tf_op jit(solution)/shard_map/all_to_all | solution.py:242
  13.4 91.3 %all-gather.3.cloned.1.call-start = ((), (), s32[]{:S(2)}) async-start(), calls=%async_computation.1 | async-start | bytes 7163904 | tf_op jit(solution)/shard_map/all_gather | solution.py:259
Sparse Core Ops, SparseCore 0:
  32.3 72.3 all-gather.2
